TPU v7x, 32 devices: a whole 2x2x4 slice. The times are simulated.
32 devices in a mesh: ctx: 8 (over z, y), head: 4 (over x, core).
Axes of the slice: x: 2, y: 2, z: 4, core: 2. Of those that a mesh axis runs over, the one named last changes fastest.
Arguments:
- queries: bfloat16 [3, 8, 8192], P(None, None, 'head'), may hold values from -8 to 8
- k_cache: bfloat16 [8, 2048, 1024], P(None, 'ctx', 'head'), may hold values from -6 to 6
- v_cache: bfloat16 [8, 2048, 1024], P(None, 'ctx', 'head'), may hold values from -6 to 6
- new_keys: bfloat16 [3, 8, 1024], P(None, None, 'head'), may hold values from -6 to 6
- new_values: bfloat16 [3, 8, 1024], P(None, None, 'head'), may hold values from -6 to 6
- fill: int32 [8, 8], P(None, 'ctx'), may hold values from 2 to 253, as said below
- owner: int32 [3, 8], replicated, may hold values from 0 to 7
- out_weight: bfloat16 [8192, 8192], P('head', 'ctx'), may hold values from -0.09375 to 0.09375
Outputs:
- keys_out: bfloat16 [8, 2048, 1024], P(None, 'ctx', 'head')
- values_out: bfloat16 [8, 2048, 1024], P(None, 'ctx', 'head')
- mixed: bfloat16 [3, 8, 8192], P(None, None, ('ctx', 'head'))
Inputs may be any that keep to these rules, and one draw needn't show every extreme that they name: Rows 0 to fill - 1 of each shard hold the sequence's earlier positions; some entry equals 253.
All inputs are finite; a program needn't handle non-finite values.
Results may differ from a plain program's by a relative error of at most 0.0051.
Values may be sent and summed in bfloat16 or wider, within the bound.
A program may use at most 128 MiB of HBM per device.

v0:
```python
import jax
import jax.numpy as jnp
from jax import lax
from jax.sharding import PartitionSpec as P

HD = 128


def on_device(queries, k_cache, v_cache, new_keys, new_values, fill, owner, out_weight):
    steps, batch = owner.shape
    rows = k_cache.shape[1]
    device_pos = lax.axis_index("ctx")
    mine = (owner == device_pos).astype(jnp.int32)
    seen = jnp.cumsum(mine, axis=0)
    local_fill = fill[:, 0]
    slot = local_fill[None, :] + seen - 1
    row_ids = lax.broadcasted_iota(jnp.int32, (batch, rows), 1)
    keys_out, values_out = (k_cache, v_cache)
    for step in range(steps):
        target = ((row_ids == slot[step][:, None]) & (mine[step][:, None] == 1))[:, :, None]
        keys_out = jnp.where(target, new_keys[step][:, None, :], keys_out)
        values_out = jnp.where(target, new_values[step][:, None, :], values_out)
    lengths = local_fill[None, :] + seen
    kv_local = keys_out.shape[2] // HD
    groups = queries.shape[2] // (kv_local * HD)
    query_heads = queries.reshape(steps, batch, kv_local, groups, HD)
    key_heads = keys_out.reshape(batch, rows, kv_local, HD)
    value_heads = values_out.reshape(batch, rows, kv_local, HD)
    scores = jnp.einsum(
        "sbgqd,brgd->sbgqr", query_heads, key_heads, preferred_element_type=jnp.float32
    ) * (1.0 / HD**0.5)
    slot_ids = lax.broadcasted_iota(jnp.int32, (1, 1, 1, 1, rows), 4)
    live = slot_ids < lengths[:, :, None, None, None]
    masked = jnp.where(live, scores, -1e30)
    peak = jnp.max(masked, axis=-1)
    weights = jnp.where(live, jnp.exp(masked - peak[..., None]), 0.0)
    total = jnp.sum(weights, axis=-1)
    rounded = weights.astype(jnp.bfloat16)
    numer = jnp.einsum(
        "sbgqr,brgd->sbgqd", rounded, value_heads, preferred_element_type=jnp.float32
    )
    largest = lax.pmax(peak, "ctx")
    factor = jnp.exp(peak - largest)
    numer_all, total_all = lax.psum((numer * factor[..., None], total * factor), "ctx")
    attention = (numer_all / total_all[..., None]).astype(jnp.bfloat16)
    attention_rows = attention.reshape(steps * batch, kv_local * groups * HD)
    partial_out = jnp.dot(attention_rows, out_weight, preferred_element_type=jnp.float32)
    mixed = lax.psum_scatter(partial_out, "head", scatter_dimension=1, tiled=True).astype(
        jnp.bfloat16
    )
    return (keys_out, values_out, mixed.reshape(steps, batch, -1))


def solution(mesh):
    in_specs = (
        P(None, None, "head"),
        P(None, "ctx", "head"),
        P(None, "ctx", "head"),
        P(None, None, "head"),
        P(None, None, "head"),
        P(None, "ctx"),
        P(),
        P("head", "ctx"),
    )
    out_specs = (P(None, "ctx", "head"), P(None, "ctx", "head"), P(None, None, ("ctx", "head")))
    return jax.shard_map(
        on_device, mesh=mesh, in_specs=in_specs, out_specs=out_specs, check_vma=False
    )
```

profile of v0, /device:TPU:0, one launch (start us, length us, event | category | flops | bytes accessed | tf_op | source)
XLA Modules:
  0.0 155.7 jit_solution(815850899702582466)
XLA Ops:
  7.2 0.0 copy-start
  7.2 0.0 all-reduce.2.cloned.1.call-start
  7.2 0.7 compare_convert_fusion
  8.0 0.7 broadcast_add_fusion
  8.6 0.1 fusion.14
  8.7 0.8 slice_bitcast_fusion.2
  9.5 0.1 fusion.12
  9.6 3.0 %select_select_fusion = (bf16[8,256,256]{2,1,0:T(8,128)(2,1)S(1)}, bf16[8,256,256]{2,1,0:T(8,128)(2,1)S(1)}) fusion(bf16[8,256,256]{2,1,0:T(8,128)(2,1)} %param.10, pred[8,256]{1,0:T(8,128)(4,1)S(1)} %fusion.14, pred[8,256]{1,0:T(8,128)(4,1)S(1)} %get-tuple-element.24, pred[8,256]{1,0:T(8,128)(4,1)S(1)} %get-tuple-element.23, ...), kind=kLoop, calls=%fused_computation.7 | loop fusion | flops 3145728 | bytes 4225024 | tf_op jit(solution)/shard_map/jit(_where)/select_n | solution.py:22
  12.5 0.0 copy-start.1
  12.5 0.0 copy-start.2
  12.6 0.3 reshape.192
  12.9 0.1 copy.15
  12.9 0.1 iota_compare_fusion
  13.0 0.0 copy-done
  13.0 1.1 fusion.17
  14.2 38.8 %pmax.7 = f32[3,8,2,8]{3,0,2,1:T(4,128)S(1)} all-reduce(f32[3,8,2,8]{3,0,2,1:T(4,128)S(1)} %get-tuple-element.21), channel_id=1, replica_groups=mesh['ctx'=8,'head'=4] {'ctx'}, use_global_device_ids=true, to_apply=%region_2.3 | all-reduce | flops 384 | bytes 3072 | tf_op jit(solution)/shard_map/pmax | solution.py:42
  53.0 1.2 fusion.5
  54.3 0.3 reshape.191
  54.6 2.0 %fusion.2 = f32[3,8,2,8,128]{4,3,0,2,1:T(8,128)} fusion(bf16[8,256,2,128,1]{3,2,1,0,4:T(2,128)(2,1)S(1)} %bitcast.43, f32[3,8,2,8,256]{4,3,0,2,1:T(8,128)} %get-tuple-element.22, f32[3,8,2,8]{3,0,2,1:T(4,128)S(1)} %get-tuple-element.21, pred[3,8,256]{2,0,1:T(4,128)(4,1)S(1)} %iota_compare_fusion, f32[3,8,2,8]{3,0,2,1:T(4,128)S(1)} %get-tuple-element.4), kind=kOutput, calls=%fused_computation.4 | convolution fusion | flops 25509888 | bytes 1647616 | tf_op jit(solution)/shard_map/sbgqr,brgd->sbgqd/dot_general | solution.py:39
  56.6 0.0 copy-done.1
  56.6 0.0 copy-done.2
  56.6 0.0 all-reduce.2.cloned.1.call-update
  56.6 0.0 reduce-scatter.2.cloned.1.call-start
  56.7 33.1 %psum.15 = f32[3,8,2,8]{3,0,2,1:T(4,128)S(1)} all-reduce(f32[3,8,2,8]{3,0,2,1:T(4,128)S(1)} %get-tuple-element.3), channel_id=1, replica_groups=mesh['ctx'=8,'head'=4] {'ctx'}, use_global_device_ids=true, to_apply=%region_5.6 | all-reduce | flops 384 | bytes 3072 | tf_op jit(solution)/shard_map/psum | solution.py:44
  89.7 34.4 %all-reduce.2.cloned.1.call-done = f32[3,8,2,8,128]{4,3,0,2,1:T(8,128)} async-done(((f32[3,8,2,8,128]{4,3,0,2,1:T(8,128)}), f32[3,8,2,8,128]{4,3,0,2,1:T(8,128)}) %all-reduce.2.cloned.1.call-update) | async-done | bytes 196624 | tf_op jit(solution)/shard_map/psum | solution.py:44
  124.1 1.0 divide_convert_fusion
  125.2 3.5 %fusion.18 = f32[24,1024]{1,0:T(8,128)} fusion(bf16[24,2048]{1,0:T(8,128)(2,1)S(1)} %reshape.194, bf16[2048,1024]{1,0:T(8,128)(2,1)} %param.15), kind=kOutput, calls=%fused_computation.44 | convolution fusion | flops 100663296 | bytes 4390912 | tf_op jit(solution)/shard_map/dot_general | solution.py:47
  128.7 0.0 reduce-scatter.2.cloned.1.call-update
  128.7 18.7 %reduce-scatter.2.cloned.1.call-done = f32[24,256]{1,0:T(8,128)} async-done(((f32[24,1024]{1,0:T(8,128)}), f32[24,256]{1,0:T(8,128)}) %reduce-scatter.2.cloned.1.call-update) | async-done | bytes 24592 | tf_op jit(solution)/shard_map/reduce_scatter | solution.py:48
  147.5 1.3 convert_bitcast_fusion
  (6 shorter events, 0.1 us)
Async XLA Ops:
  7.2 5.9 %copy-start = (bf16[3,8,2048]{2,1,0:T(8,128)(2,1)S(1)}, bf16[3,8,2048]{2,1,0:T(8,128)(2,1)}, u32[]{:S(2)}) copy-start(bf16[3,8,2048]{2,1,0:T(8,128)(2,1)} %param.8) | copy-start | bytes 294916
  7.2 116.9 %all-reduce.2.cloned.1.call-start = ((), (), s32[]{:S(2)}) async-start(), calls=%async_computation.1 | async-start | bytes 393216 | tf_op jit(solution)/shard_map/psum | solution.py:44
  12.5 44.1 %copy-start.1 = (bf16[8,256,256]{2,1,0:T(8,128)(2,1)}, bf16[8,256,256]{2,1,0:T(8,128)(2,1)S(1)}, u32[]{:S(2)}) copy-start(bf16[8,256,256]{2,1,0:T(8,128)(2,1)S(1)} %get-tuple-element.13) | copy-start | bytes 3145732
  12.5 44.1 %copy-start.2 = (bf16[8,256,256]{2,1,0:T(8,128)(2,1)}, bf16[8,256,256]{2,1,0:T(8,128)(2,1)S(1)}, u32[]{:S(2)}) copy-start(bf16[8,256,256]{2,1,0:T(8,128)(2,1)S(1)} %get-tuple-element.14) | copy-start | bytes 3145732
  56.6 90.9 %reduce-scatter.2.cloned.1.call-start = ((), (), s32[]{:S(2)}) async-start(), calls=%async_computation.2 | async-start | bytes 122880 | tf_op jit(solution)/shard_map/reduce_scatter | solution.py:48
Sparse Core Ops, SparseCore 0:
  56.8 67.3 all-reduce.1
  128.9 18.5 reduce-scatter.1
where the time goes:
time: 156 us
  blocking collectives  71.9 us (46%)
  waiting for transfers between devices  53.1 us (34%)
  between operations  14.1 us (9%)
  other arithmetic  8.24 us (5%)
  matrix products  6.62 us (4%)
    pmax x1, blocking collectives, on_device(): largest = lax.pmax(peak, 'ctx')  38.8 us
    psum x1, waiting for transfers between devices, on_device(): lax.psum((numer * factor[..., None], total * factor), 'ctx')  34.4 us
    psum x1, blocking collectives, on_device(): lax.psum((numer * factor[..., None], total * factor), 'ctx')  33.1 us
    reduce_scatter x1, waiting for transfers between devices, on_device(): lax.psum_scatter(partial_out, 'head', scatter_dimension=1, tiled=True)  18.7 us
    dot_general x1, matrix products, on_device(): jnp.dot(attention_rows, out_weight, preferred_element_type=jnp.float32)  3.47 us
  transfers between devices with their start and end apart: 2, of which 2 were waited for; matrix products, arithmetic and copies ran while one was open for 0% of the time, Pallas kernels for 0%

commit v1 on v0

--- a/solution.py
+++ b/solution.py
@@ -1,6 +1,10 @@
+import functools
+
 import jax
 import jax.numpy as jnp
 from jax import lax
+from jax.experimental import pallas as pl
+from jax.experimental.pallas import tpu as pltpu
 from jax.sharding import PartitionSpec as P
 
 HD = 128
@@ -51,6 +55,314 @@
     return (keys_out, values_out, mixed.reshape(steps, batch, -1))
 
 
+MESH = pl.DeviceIdType.MESH
+STAT_ROWS = 16
+
+
+def new_rows(old, slots, rows_f32, step_rows):
+    ids = lax.broadcasted_iota(jnp.int32, old.shape, 0)
+    out = old.astype(jnp.float32)
+    for slot, row in zip(slots, step_rows):
+        out = jnp.where(ids == slot, rows_f32[row : row + 1, :], out)
+    return out.astype(old.dtype)
+
+
+def fused_kernel(
+    n_ctx, n_head, steps, batch, groups, kv_local,
+    fill, owner, q_hbm, k_hbm, v_hbm, nk_hbm, nv_hbm, w_hbm,
+    k_out, v_out, mixed,
+    q_v, nk_v, nv_v, k_v, v_v, w_v, q_rows, part, stat, nk_f, nv_f,
+    send1, recv1, send2, recv2, send3, recv3,
+    small_sem, k_sem, v_sem, w_sem, ko_sem, vo_sem,
+    ssem1, rsem1, ssem2, rsem2, ssem3, rsem3,
+):
+    me = lax.axis_index("ctx")
+    hme = lax.axis_index("head")
+    tokens = steps * batch
+    rows = k_v.shape[1]
+    heads = groups * kv_local
+    per = heads // n_ctx
+    block = per * tokens
+    depth = per * HD
+    width = mixed.shape[2]
+
+    barrier = pltpu.get_barrier_semaphore()
+    for d in range(1, n_ctx):
+        pl.semaphore_signal(barrier, inc=1, device_id={"ctx": lax.rem(me + d, n_ctx)}, device_id_type=MESH)
+    for d in range(1, n_head):
+        pl.semaphore_signal(barrier, inc=1, device_id={"head": lax.rem(hme + d, n_head)}, device_id_type=MESH)
+
+    smalls = [
+        pltpu.make_async_copy(q_hbm, q_v, small_sem.at[0]),
+        pltpu.make_async_copy(nk_hbm, nk_v, small_sem.at[1]),
+        pltpu.make_async_copy(nv_hbm, nv_v, small_sem.at[2]),
+    ]
+    k_in = [pltpu.make_async_copy(k_hbm.at[b], k_v.at[b], k_sem.at[b]) for b in range(batch)]
+    v_in = [pltpu.make_async_copy(v_hbm.at[b], v_v.at[b], v_sem.at[b]) for b in range(batch)]
+    w_in = [
+        pltpu.make_async_copy(w_hbm.at[pl.ds(c * depth, depth), :], w_v.at[c], w_sem.at[c])
+        for c in range(n_ctx)
+    ]
+    for copy in smalls:
+        copy.start()
+    for b in range(batch):
+        k_in[b].start()
+        v_in[b].start()
+    for copy in w_in:
+        copy.start()
+
+    smalls[0].wait()
+    for s in range(steps):
+        q_f = q_v[s].astype(jnp.float32)
+        for h in range(heads):
+            q_rows[h * tokens + s * batch : h * tokens + (s + 1) * batch, :] = q_f[:, h * HD : (h + 1) * HD]
+    smalls[1].wait()
+    smalls[2].wait()
+    for s in range(steps):
+        nk_f[s * batch : (s + 1) * batch, :] = nk_v[s].astype(jnp.float32)
+        nv_f[s * batch : (s + 1) * batch, :] = nv_v[s].astype(jnp.float32)
+
+    live_rows = groups * steps
+    step_ids = lax.rem(lax.broadcasted_iota(jnp.int32, (live_rows, rows), 0), steps)
+    slot_ids = lax.broadcasted_iota(jnp.int32, (live_rows, rows), 1)
+    lane = lax.broadcasted_iota(jnp.int32, (live_rows, HD), 1)
+    pick = (
+        lax.broadcasted_iota(jnp.int32, (STAT_ROWS, HD), 0)
+        == lax.broadcasted_iota(jnp.int32, (STAT_ROWS, HD), 1)
+    ).astype(jnp.bfloat16)
+
+    slots, lengths = [], []
+    for b in range(batch):
+        seen = fill[b, 0]
+        slots_b, lengths_b = [], []
+        for s in range(steps):
+            mine = owner[s, b] == me
+            slots_b.append(jnp.where(mine, seen, -1))
+            seen = seen + jnp.where(mine, 1, 0)
+            lengths_b.append(seen)
+        slots.append(slots_b)
+        lengths.append(lengths_b)
+
+    first = [
+        [
+            pltpu.make_async_remote_copy(
+                src_ref=send1.at[c],
+                dst_ref=recv1.at[lax.rem(c - me + n_ctx, n_ctx)],
+                send_sem=ssem1.at[c],
+                recv_sem=rsem1.at[lax.rem(c - me + n_ctx, n_ctx)],
+                device_id={"ctx": c},
+                device_id_type=MESH,
+            )
+        ]
+        for c in range(n_ctx)
+    ]
+    sent = 0
+    for g in range(kv_local):
+        cols = slice(g * HD, (g + 1) * HD)
+        nk_g, nv_g = nk_f[:, cols], nv_f[:, cols]
+        for b in range(batch):
+            at = pl.ds(g * groups * tokens + b, live_rows, stride=batch)
+            step_rows = [s * batch + b for s in range(steps)]
+            if g == 0:
+                k_in[b].wait()
+                v_in[b].wait()
+            keys = new_rows(k_v[b, :, cols], slots[b], nk_g, step_rows)
+            values = new_rows(v_v[b, :, cols], slots[b], nv_g, step_rows)
+            k_v[b, :, cols] = keys
+            v_v[b, :, cols] = values
+            if g == kv_local - 1:
+                pltpu.make_async_copy(k_v.at[b], k_out.at[b], ko_sem.at[b]).start()
+                pltpu.make_async_copy(v_v.at[b], v_out.at[b], vo_sem.at[b]).start()
+            query = q_rows[at, :].astype(jnp.bfloat16)
+            scores = lax.dot_general(
+                query, keys, (((1,), (1,)), ((), ())), preferred_element_type=jnp.float32
+            ) * (1.0 / HD**0.5)
+            length = jnp.full((live_rows, rows), lengths[b][steps - 1], jnp.int32)
+            for s in range(steps - 1):
+                length = jnp.where(step_ids == s, lengths[b][s], length)
+            live = slot_ids < length
+            masked = jnp.where(live, scores, -1e30)
+            peak = jnp.max(masked, axis=1, keepdims=True)
+            weights = jnp.where(live, jnp.exp(masked - peak), 0.0)
+            total = jnp.sum(weights, axis=1, keepdims=True)
+            part[at, :] = jnp.dot(
+                weights.astype(jnp.bfloat16), values, preferred_element_type=jnp.float32
+            )
+            both = jnp.where(lax.rem(lane, 2) == 0, peak, total)
+            high = both.astype(jnp.bfloat16).astype(jnp.float32)
+            middle = (both - high).astype(jnp.bfloat16).astype(jnp.float32)
+            low = both - high - middle
+            stat[at, :] = jnp.where(lane < 2, high, jnp.where(lane < 4, middle, low))
+        if g == 0:
+            pl.semaphore_wait(barrier, n_ctx + n_head - 2)
+        ready = n_ctx * (g + 1) // kv_local
+        for c in range(sent, ready):
+            here = slice(c * block, (c + 1) * block)
+            send1[c, 0:block, :] = part[here, :].astype(jnp.bfloat16)
+            turned = lax.dot_general(
+                pick, stat[here, :].astype(jnp.bfloat16), (((1,), (1,)), ((), ())),
+                preferred_element_type=jnp.float32,
+            )
+            send1[c, block : block + STAT_ROWS, 0:block] = turned.astype(jnp.bfloat16)
+
+            @pl.when(me != c)
+            def _():
+                first[c][0].start()
+
+        sent = ready
+
+    recv1[0] = send1[me]
+    for d in range(1, n_ctx):
+        pltpu.make_async_remote_copy(
+            src_ref=send1.at[0], dst_ref=recv1.at[d], send_sem=ssem1.at[0], recv_sem=rsem1.at[d],
+            device_id={"ctx": lax.rem(me + d, n_ctx)}, device_id_type=MESH,
+        ).wait_recv()
+    peaks, totals = [], []
+    for d in range(n_ctx):
+        got = recv1[d, block : block + STAT_ROWS, 0:block].astype(jnp.float32)
+        peaks.append(got[0:1] + got[2:3] + got[4:5])
+        totals.append(got[1:2] + got[3:4] + got[5:6])
+    peaks = jnp.concatenate(peaks, axis=0)
+    totals = jnp.concatenate(totals, axis=0)
+    factor = jnp.exp(peaks - jnp.max(peaks, axis=0, keepdims=True))
+    shares = factor / jnp.sum(factor * totals, axis=0, keepdims=True)
+    shares = jnp.transpose(shares)
+    attention = jnp.zeros((block, HD), jnp.float32)
+    for d in range(n_ctx):
+        attention += recv1[d, 0:block, :].astype(jnp.float32) * shares[:, d : d + 1]
+    send2[...] = attention.astype(jnp.bfloat16)
+
+    second = []
+    for d in range(1, n_ctx):
+        copy = pltpu.make_async_remote_copy(
+            src_ref=send2, dst_ref=recv2.at[d], send_sem=ssem2.at[d], recv_sem=rsem2.at[d],
+            device_id={"ctx": lax.rem(me + d, n_ctx)}, device_id_type=MESH,
+        )
+        copy.start()
+        second.append(copy)
+    for copy in w_in:
+        copy.wait()
+    share = None
+    for d in range(n_ctx):
+        if d > 0:
+            second[d - 1].wait_recv()
+            got = recv2[d].astype(jnp.float32)
+        else:
+            got = send2[...].astype(jnp.float32)
+        features = jnp.concatenate(
+            [got[i * tokens : (i + 1) * tokens] for i in range(per)], axis=1
+        ).astype(jnp.bfloat16)
+        product = jnp.dot(
+            features, w_v[lax.rem(me - d + n_ctx, n_ctx)], preferred_element_type=jnp.float32
+        )
+        share = product if share is None else share + product
+    for h in range(n_head):
+        send3[h] = share[:, h * width : (h + 1) * width]
+    third = []
+    for d in range(1, n_head):
+        target = lax.rem(hme + d, n_head)
+        copy = pltpu.make_async_remote_copy(
+            src_ref=send3.at[target], dst_ref=recv3.at[d], send_sem=ssem3.at[d], recv_sem=rsem3.at[d],
+            device_id={"head": target}, device_id_type=MESH,
+        )
+        copy.start()
+        third.append(copy)
+    result = send3[hme]
+    for copy in third:
+        copy.wait_recv()
+    for d in range(1, n_head):
+        result += recv3[d]
+    result = result.astype(mixed.dtype)
+    for s in range(steps):
+        mixed[s] = result[s * batch : (s + 1) * batch]
+
+    for c in range(n_ctx):
+
+        @pl.when(me != c)
+        def _():
+            first[c][0].wait_send()
+
+    for copy in second:
+        copy.wait_send()
+    for copy in third:
+        copy.wait_send()
+    for b in range(batch):
+        pltpu.make_async_copy(k_v.at[b], k_out.at[b], ko_sem.at[b]).wait()
+        pltpu.make_async_copy(v_v.at[b], v_out.at[b], vo_sem.at[b]).wait()
+
+
+def on_device_fused(
+    n_ctx, n_head, queries, k_cache, v_cache, new_keys, new_values, fill, owner, out_weight
+):
+    steps, batch, features = queries.shape
+    rows, kv_width = k_cache.shape[1:]
+    kv_local = kv_width // HD
+    heads = features // HD
+    tokens = steps * batch
+    columns = out_weight.shape[1]
+    per = heads // n_ctx
+    block = per * tokens
+    if heads % n_ctx or block % 16 or block > HD or n_ctx % kv_local or batch != 8 or columns % (n_head * HD):
+        return on_device(
+            queries, k_cache, v_cache, new_keys, new_values, fill, owner, out_weight
+        )
+    kernel = functools.partial(
+        fused_kernel, n_ctx, n_head, steps, batch, heads // kv_local, kv_local
+    )
+    whole = pl.BlockSpec(memory_space=pl.ANY)
+    scalars = pl.BlockSpec(memory_space=pltpu.SMEM)
+    dma = pltpu.SemaphoreType.DMA
+    return pl.pallas_call(
+        kernel,
+        out_shape=(
+            jax.ShapeDtypeStruct(k_cache.shape, k_cache.dtype),
+            jax.ShapeDtypeStruct(v_cache.shape, v_cache.dtype),
+            jax.ShapeDtypeStruct((steps, batch, columns // n_head), jnp.bfloat16),
+        ),
+        in_specs=[scalars, scalars] + [whole] * 6,
+        out_specs=(whole, whole, pl.BlockSpec(memory_space=pltpu.VMEM)),
+        scratch_shapes=[
+            pltpu.VMEM(queries.shape, jnp.bfloat16),
+            pltpu.VMEM(new_keys.shape, jnp.bfloat16),
+            pltpu.VMEM(new_values.shape, jnp.bfloat16),
+            pltpu.VMEM(k_cache.shape, jnp.bfloat16),
+            pltpu.VMEM(v_cache.shape, jnp.bfloat16),
+            pltpu.VMEM((n_ctx, per * HD, columns), jnp.bfloat16),
+            pltpu.VMEM((heads * tokens, HD), jnp.float32),
+            pltpu.VMEM((heads * tokens, HD), jnp.float32),
+            pltpu.VMEM((heads * tokens, HD), jnp.float32),
+            pltpu.VMEM((tokens, kv_width), jnp.float32),
+            pltpu.VMEM((tokens, kv_width), jnp.float32),
+            pltpu.VMEM((n_ctx, block + STAT_ROWS, HD), jnp.bfloat16),
+            pltpu.VMEM((n_ctx, block + STAT_ROWS, HD), jnp.bfloat16),
+            pltpu.VMEM((block, HD), jnp.bfloat16),
+            pltpu.VMEM((n_ctx, block, HD), jnp.bfloat16),
+            pltpu.VMEM((n_head, tokens, columns // n_head), jnp.float32),
+            pltpu.VMEM((n_head, tokens, columns // n_head), jnp.float32),
+            dma((3,)),
+            dma((batch,)),
+            dma((batch,)),
+            dma((n_ctx,)),
+            dma((batch,)),
+            dma((batch,)),
+            dma((n_ctx,)),
+            dma((n_ctx,)),
+            dma((n_ctx,)),
+            dma((n_ctx,)),
+            dma((n_head,)),
+            dma((n_head,)),
+        ],
+        compiler_params=pltpu.CompilerParams(
+            collective_id=0, has_side_effects=True, vmem_limit_bytes=48 * 1024 * 1024
+        ),
+        cost_estimate=pl.CostEstimate(
+            flops=2 * tokens * features * (columns + 2 * rows),
+            bytes_accessed=2 * (2 * k_cache.size + 2 * v_cache.size + out_weight.size),
+            transcendentals=tokens * heads * rows,
+        ),
+    )(fill, owner, queries, k_cache, v_cache, new_keys, new_values, out_weight)
+
+
 def solution(mesh):
     in_specs = (
         P(None, None, "head"),
@@ -64,5 +376,5 @@
     )
     out_specs = (P(None, "ctx", "head"), P(None, "ctx", "head"), P(None, None, ("ctx", "head")))
     return jax.shard_map(
-        on_device, mesh=mesh, in_specs=in_specs, out_specs=out_specs, check_vma=False
-    )
+        functools.partial(on_device_fused, mesh.shape["ctx"], mesh.shape["head"]), mesh=mesh, in_specs=in_specs, out_specs=out_specs, check_vma=False
+    )

time: 156 us -> 41.2 us (0.26)
  blocking collectives: 71.9 us -> 0 us
  waiting for transfers between devices: 53.1 us -> 0 us
  Pallas kernels: 0 us -> 31.5 us
  between operations: 14.1 us -> 0.65 us
  other arithmetic: 8.24 us -> 0 us
  local copies, waits for them, and re-layouts: 1.53 us -> 8.71 us
  matrix products: 6.62 us -> 0 us
    pmax x1 -> x0, blocking collectives: 38.8 us -> none  [on_device(): largest = lax.pmax(peak, 'ctx')]
    psum x1 -> x0, waiting for transfers between devices: 34.4 us -> none  [on_device(): lax.psum((numer * factor[..., None], total * factor), 'ctx')]
    psum x1 -> x0, blocking collectives: 33.1 us -> none  [on_device(): lax.psum((numer * factor[..., None], total * factor), 'ctx')]
    pallas_call x0 -> x1, Pallas kernels: none -> 31.5 us  [on_device_fused(): pl.pallas_call(kernel, out_shape=(jax.ShapeDtypeStruct(k_cache.shape, k_c...]
    reduce_scatter x1 -> x0, waiting for transfers between devices: 18.7 us -> none  [on_device(): lax.psum_scatter(partial_out, 'head', scatter_dimension=1, tiled=True)]
    unnamed x6 -> x16, local copies, waits for them, and re-layouts: 0.02 us -> 8.71 us
    dot_general x3 -> x0, matrix products: 6.62 us -> none  [the longest x1 3.47 us: on_device(): jnp.dot(attention_rows, out_weight, preferred_element_type=jnp.float32)]
    select_n x1 -> x0, other arithmetic: 2.97 us -> none  [on_device(): values_out = jnp.where(target, new_values[step][:, None, :], values_out)]
  transfers between devices with their start and end apart: 2 -> 0, of which waited for: 2 -> 0; matrix products, arithmetic and copies ran while one was open for 0% -> 0% of each run, Pallas kernels for 0% -> 0%
where the time goes in v1:
time: 41.2 us; the launch traced here: 40.9 us
  Pallas kernels  31.5 us (76%)
  local copies, waits for them, and re-layouts  8.71 us (21%)
  between operations  0.65 us (2%)
    pallas_call x1, Pallas kernels, on_device_fused(): pl.pallas_call(kernel, out_shape=(jax.ShapeDtypeStruct(k_cache.shape, k_c...  31.5 us
    unnamed x16, local copies, waits for them, and re-layouts  8.71 us

profile of v1, /device:TPU:0, one launch (start us, length us, event | category | flops | bytes accessed | tf_op | source)
XLA Modules:
  0.0 40.9 jit_solution(12166201183122261477)
XLA Ops:
  0.6 0.7 %copy.11.fill = s32[8,1]{1,0:T(8,128)S(1)} copy(s32[8,1]{0,1:T(1,128)} %param.13) | data formatting | bytes 64 | tf_op args[5]
  1.4 0.0 copy-start
  1.4 1.2 %copy-done = bf16[8,256,256]{2,1,0:T(8,128)(2,1)S(1)} copy-done((bf16[8,256,256]{2,1,0:T(8,128)(2,1)S(1)}, bf16[8,256,256]{2,1,0:T(8,128)(2,1)}, u32[]{:S(2)}) %copy-start) | copy-done | bytes 1048600
  2.6 0.0 copy-start.1
  2.6 1.2 %copy-done.1 = bf16[8,256,256]{2,1,0:T(8,128)(2,1)S(1)} copy-done((bf16[8,256,256]{2,1,0:T(8,128)(2,1)S(1)}, bf16[8,256,256]{2,1,0:T(8,128)(2,1)}, u32[]{:S(2)}) %copy-start.1) | copy-done | bytes 1048600
  3.8 0.0 copy-start.2
  3.8 0.9 %copy-done.2 = bf16[3,8,2048]{2,1,0:T(8,128)(2,1)S(1)} copy-done((bf16[3,8,2048]{2,1,0:T(8,128)(2,1)S(1)}, bf16[3,8,2048]{2,1,0:T(8,128)(2,1)}, u32[]{:S(2)}) %copy-start.2) | copy-done | bytes 98328
  4.7 0.0 copy-start.3
  4.7 0.7 %copy-done.3 = bf16[3,8,256]{2,1,0:T(8,128)(2,1)S(1)} copy-done((bf16[3,8,256]{2,1,0:T(8,128)(2,1)S(1)}, bf16[3,8,256]{2,1,0:T(8,128)(2,1)}, u32[]{:S(2)}) %copy-start.3) | copy-done | bytes 12312
  5.4 0.0 copy-start.4
  5.4 0.7 %copy-done.4 = bf16[3,8,256]{2,1,0:T(8,128)(2,1)S(1)} copy-done((bf16[3,8,256]{2,1,0:T(8,128)(2,1)S(1)}, bf16[3,8,256]{2,1,0:T(8,128)(2,1)}, u32[]{:S(2)}) %copy-start.4) | copy-done | bytes 12312
  6.1 0.0 copy-start.5
  6.1 0.7 %copy-done.5 = s32[3,8]{1,0:T(4,128)S(1)} copy-done((s32[3,8]{1,0:T(4,128)S(1)}, s32[3,8]{1,0:T(4,128)}, u32[]{:S(2)}) %copy-start.5) | copy-done | bytes 120
  6.8 31.5 %shard_map.103 = (bf16[8,256,256]{2,1,0:T(8,128)(2,1)S(1)}, bf16[8,256,256]{2,1,0:T(8,128)(2,1)S(1)}, bf16[3,8,256]{2,1,0:T(8,128)(2,1)S(1)}) custom-call(s32[8,1]{1,0:T(8,128)S(1)} %copy.11.fill, s32[3,8]{1,0:T(4,128)S(1)} %copy-done.5, bf16[3,8,2048]{2,1,0:T(8,128)(2,1)S(1)} %copy-done.2, bf16[8,256,256]{2,1,0:T(8,128)(2,1)S(1)} %copy-done, ...), custom_call_target="tpu_custom_call" | custom-call | flops 150994944 | bytes 8388608 | tf_op jit(solution)/shard_map/pallas_call | solution.py:315
  38.3 1.0 %copy.15 = bf16[8,256,256]{2,1,0:T(8,128)(2,1)} copy(bf16[8,256,256]{2,1,0:T(8,128)(2,1)S(1)} %get-tuple-element.6) | data formatting | bytes 2097152
  39.3 1.0 %copy.16 = bf16[8,256,256]{2,1,0:T(8,128)(2,1)} copy(bf16[8,256,256]{2,1,0:T(8,128)(2,1)S(1)} %get-tuple-element.7) | data formatting | bytes 2097152
  40.3 0.6 %copy.17 = bf16[3,8,256]{2,1,0:T(8,128)(2,1)} copy(bf16[3,8,256]{2,1,0:T(8,128)(2,1)S(1)} %get-tuple-element.8) | data formatting | bytes 24576
Async XLA Ops:
  1.4 1.2 %copy-start = (bf16[8,256,256]{2,1,0:T(8,128)(2,1)S(1)}, bf16[8,256,256]{2,1,0:T(8,128)(2,1)}, u32[]{:S(2)}) copy-start(bf16[8,256,256]{2,1,0:T(8,128)(2,1)} %k_hbm.1) | copy-start | bytes 3145732
  2.6 1.2 %copy-start.1 = (bf16[8,256,256]{2,1,0:T(8,128)(2,1)S(1)}, bf16[8,256,256]{2,1,0:T(8,128)(2,1)}, u32[]{:S(2)}) copy-start(bf16[8,256,256]{2,1,0:T(8,128)(2,1)} %v_hbm.1) | copy-start | bytes 3145732
  3.8 0.9 %copy-start.2 = (bf16[3,8,2048]{2,1,0:T(8,128)(2,1)S(1)}, bf16[3,8,2048]{2,1,0:T(8,128)(2,1)}, u32[]{:S(2)}) copy-start(bf16[3,8,2048]{2,1,0:T(8,128)(2,1)} %q_hbm.1) | copy-start | bytes 294916
  4.7 0.7 %copy-start.3 = (bf16[3,8,256]{2,1,0:T(8,128)(2,1)S(1)}, bf16[3,8,256]{2,1,0:T(8,128)(2,1)}, u32[]{:S(2)}) copy-start(bf16[3,8,256]{2,1,0:T(8,128)(2,1)} %nk_hbm.1) | copy-start | bytes 36868
  5.4 0.7 %copy-start.4 = (bf16[3,8,256]{2,1,0:T(8,128)(2,1)S(1)}, bf16[3,8,256]{2,1,0:T(8,128)(2,1)}, u32[]{:S(2)}) copy-start(bf16[3,8,256]{2,1,0:T(8,128)(2,1)} %nv_hbm.1) | copy-start | bytes 36868
  6.1 0.7 %copy-start.5 = (s32[3,8]{1,0:T(4,128)S(1)}, s32[3,8]{1,0:T(4,128)}, u32[]{:S(2)}) copy-start(s32[3,8]{1,0:T(4,128)} %owner.1) | copy-start | bytes 292

commit v2 on v1

--- a/solution.py
+++ b/solution.py
@@ -57,6 +57,7 @@
 
 MESH = pl.DeviceIdType.MESH
 STAT_ROWS = 16
+VMEM_BYTES = 64 * 1024 * 1024
 
 
 def new_rows(old, slots, rows_f32, step_rows):
@@ -133,7 +134,7 @@
 
     slots, lengths = [], []
     for b in range(batch):
-        seen = fill[b, 0]
+        seen = fill[b]
         slots_b, lengths_b = [], []
         for s in range(steps):
             mine = owner[s, b] == me
@@ -143,58 +144,61 @@
         slots.append(slots_b)
         lengths.append(lengths_b)
 
-    first = [
-        [
-            pltpu.make_async_remote_copy(
-                src_ref=send1.at[c],
-                dst_ref=recv1.at[lax.rem(c - me + n_ctx, n_ctx)],
-                send_sem=ssem1.at[c],
-                recv_sem=rsem1.at[lax.rem(c - me + n_ctx, n_ctx)],
-                device_id={"ctx": c},
-                device_id_type=MESH,
-            )
-        ]
-        for c in range(n_ctx)
-    ]
+    def first(c):
+        d = lax.rem(c - me + n_ctx, n_ctx)
+        return pltpu.make_async_remote_copy(
+            src_ref=send1.at[c], dst_ref=recv1.at[d], send_sem=ssem1.at[c], recv_sem=rsem1.at[d],
+            device_id={"ctx": c}, device_id_type=MESH,
+        )
+
+    for b in range(batch):
+        k_in[b].wait()
+    for b in range(batch):
+        v_in[b].wait()
+    all_b = range(batch)
     sent = 0
     for g in range(kv_local):
         cols = slice(g * HD, (g + 1) * HD)
         nk_g, nv_g = nk_f[:, cols], nv_f[:, cols]
-        for b in range(batch):
-            at = pl.ds(g * groups * tokens + b, live_rows, stride=batch)
-            step_rows = [s * batch + b for s in range(steps)]
-            if g == 0:
-                k_in[b].wait()
-                v_in[b].wait()
-            keys = new_rows(k_v[b, :, cols], slots[b], nk_g, step_rows)
-            values = new_rows(v_v[b, :, cols], slots[b], nv_g, step_rows)
-            k_v[b, :, cols] = keys
-            v_v[b, :, cols] = values
-            if g == kv_local - 1:
-                pltpu.make_async_copy(k_v.at[b], k_out.at[b], ko_sem.at[b]).start()
-                pltpu.make_async_copy(v_v.at[b], v_out.at[b], vo_sem.at[b]).start()
-            query = q_rows[at, :].astype(jnp.bfloat16)
-            scores = lax.dot_general(
-                query, keys, (((1,), (1,)), ((), ())), preferred_element_type=jnp.float32
-            ) * (1.0 / HD**0.5)
+        at = [pl.ds(g * groups * tokens + b, live_rows, stride=batch) for b in all_b]
+        step_rows = [[s * batch + b for s in range(steps)] for b in all_b]
+        query = [q_rows[at[b], :].astype(jnp.bfloat16) for b in all_b]
+        keys = [new_rows(k_v[b, :, cols], slots[b], nk_g, step_rows[b]) for b in all_b]
+        scores = [
+            lax.dot_general(
+                query[b], keys[b], (((1,), (1,)), ((), ())), preferred_element_type=jnp.float32
+            )
+            for b in all_b
+        ]
+        for b in all_b:
+            k_v[b, :, cols] = keys[b]
+        values = [new_rows(v_v[b, :, cols], slots[b], nv_g, step_rows[b]) for b in all_b]
+        for b in all_b:
+            v_v[b, :, cols] = values[b]
+        live = []
+        for b in all_b:
             length = jnp.full((live_rows, rows), lengths[b][steps - 1], jnp.int32)
             for s in range(steps - 1):
                 length = jnp.where(step_ids == s, lengths[b][s], length)
-            live = slot_ids < length
-            masked = jnp.where(live, scores, -1e30)
-            peak = jnp.max(masked, axis=1, keepdims=True)
-            weights = jnp.where(live, jnp.exp(masked - peak), 0.0)
-            total = jnp.sum(weights, axis=1, keepdims=True)
-            part[at, :] = jnp.dot(
-                weights.astype(jnp.bfloat16), values, preferred_element_type=jnp.float32
+            live.append(slot_ids < length)
+        masked = [jnp.where(live[b], scores[b] * (1.0 / HD**0.5), -1e30) for b in all_b]
+        peak = [jnp.max(masked[b], axis=1, keepdims=True) for b in all_b]
+        weights = [jnp.where(live[b], jnp.exp(masked[b] - peak[b]), 0.0) for b in all_b]
+        total = [jnp.sum(weights[b], axis=1, keepdims=True) for b in all_b]
+        sums = [
+            jnp.dot(
+                weights[b].astype(jnp.bfloat16), values[b], preferred_element_type=jnp.float32
             )
-            both = jnp.where(lax.rem(lane, 2) == 0, peak, total)
+            for b in all_b
+        ]
+        for b in all_b:
+            part[at[b], :] = sums[b]
+        for b in all_b:
+            both = jnp.where(lax.rem(lane, 2) == 0, peak[b], total[b])
             high = both.astype(jnp.bfloat16).astype(jnp.float32)
             middle = (both - high).astype(jnp.bfloat16).astype(jnp.float32)
             low = both - high - middle
-            stat[at, :] = jnp.where(lane < 2, high, jnp.where(lane < 4, middle, low))
-        if g == 0:
-            pl.semaphore_wait(barrier, n_ctx + n_head - 2)
+            stat[at[b], :] = jnp.where(lane < 2, high, jnp.where(lane < 4, middle, low))
         ready = n_ctx * (g + 1) // kv_local
         for c in range(sent, ready):
             here = slice(c * block, (c + 1) * block)
@@ -204,13 +208,20 @@
                 preferred_element_type=jnp.float32,
             )
             send1[c, block : block + STAT_ROWS, 0:block] = turned.astype(jnp.bfloat16)
+        if g == 0:
+            pl.semaphore_wait(barrier, n_ctx + n_head - 2)
+        for c in range(sent, ready):
 
             @pl.when(me != c)
-            def _():
-                first[c][0].start()
+            def _(c=c):
+                first(c).start()
 
         sent = ready
 
+    outs = [pltpu.make_async_copy(k_v.at[b], k_out.at[b], ko_sem.at[b]) for b in all_b]
+    outs += [pltpu.make_async_copy(v_v.at[b], v_out.at[b], vo_sem.at[b]) for b in all_b]
+    for copy in outs:
+        copy.start()
     recv1[0] = send1[me]
     for d in range(1, n_ctx):
         pltpu.make_async_remote_copy(
@@ -279,16 +290,15 @@
     for c in range(n_ctx):
 
         @pl.when(me != c)
-        def _():
-            first[c][0].wait_send()
+        def _(c=c):
+            first(c).wait_send()
 
     for copy in second:
         copy.wait_send()
     for copy in third:
         copy.wait_send()
-    for b in range(batch):
-        pltpu.make_async_copy(k_v.at[b], k_out.at[b], ko_sem.at[b]).wait()
-        pltpu.make_async_copy(v_v.at[b], v_out.at[b], vo_sem.at[b]).wait()
+    for copy in outs:
+        copy.wait()
 
 
 def on_device_fused(
@@ -353,14 +363,14 @@
             dma((n_head,)),
         ],
         compiler_params=pltpu.CompilerParams(
-            collective_id=0, has_side_effects=True, vmem_limit_bytes=48 * 1024 * 1024
+            collective_id=0, has_side_effects=True, vmem_limit_bytes=VMEM_BYTES
         ),
         cost_estimate=pl.CostEstimate(
             flops=2 * tokens * features * (columns + 2 * rows),
             bytes_accessed=2 * (2 * k_cache.size + 2 * v_cache.size + out_weight.size),
             transcendentals=tokens * heads * rows,
         ),
-    )(fill, owner, queries, k_cache, v_cache, new_keys, new_values, out_weight)
+    )(fill.reshape(batch), owner, queries, k_cache, v_cache, new_keys, new_values, out_weight)
 
 
 def solution(mesh):

time: 41.2 us -> 28.9 us (0.70)
  Pallas kernels: 31.5 us -> 23 us
  local copies, waits for them, and re-layouts: 8.71 us -> 5.13 us
    pallas_call x1, Pallas kernels: 31.5 us -> 23 us  [on_device_fused(): pl.pallas_call(kernel, out_shape=(jax.ShapeDtypeStruct(k_cache.shape, k_c...]
    unnamed x16 -> x5, local copies, waits for them, and re-layouts: 8.71 us -> 5.13 us
where the time goes in v2:
time: 28.9 us; the launch traced here: 28.7 us
  Pallas kernels  23 us (80%)
  local copies, waits for them, and re-layouts  5.13 us (18%)
  between operations  0.65 us (2%)
    pallas_call x1, Pallas kernels, on_device_fused(): pl.pallas_call(kernel, out_shape=(jax.ShapeDtypeStruct(k_cache.shape, k_c...  23 us
    unnamed x5, local copies, waits for them, and re-layouts  5.13 us

profile of v2, /device:TPU:0, one launch (start us, length us, event | category | flops | bytes accessed | tf_op | source)
XLA Modules:
  0.0 28.7 jit_solution(1671730199536978373)
XLA Ops:
  0.6 23.0 %shard_map.103 = (bf16[8,256,256]{2,1,0:T(8,128)(2,1)}, bf16[8,256,256]{2,1,0:T(8,128)(2,1)}, bf16[3,8,256]{2,1,0:T(8,128)(2,1)}) custom-call(s32[8]{0:T(128)} %bitcast.1, s32[3,8]{1,0:T(4,128)} %owner.1, bf16[3,8,2048]{2,1,0:T(8,128)(2,1)} %q_hbm.1, bf16[8,256,256]{2,1,0:T(8,128)(2,1)} %k_hbm.1, bf16[8,256,256]{2,1,0:T(8,128)(2,1)} %v_hbm.1, ...), custom_call_target="tpu_custom_call" | custom-call | flops 150994944 | bytes 8388608 | tf_op jit(solution)/shard_map/pallas_call | solution.py:325
  23.6 0.0 copy-start
  23.6 2.3 %copy.14 = bf16[8,256,256]{2,1,0:T(8,128)(2,1)} copy(bf16[8,256,256]{2,1,0:T(8,128)(2,1)} %get-tuple-element.6) | data formatting | bytes 2097152
  25.9 2.3 %copy.15 = bf16[8,256,256]{2,1,0:T(8,128)(2,1)} copy(bf16[8,256,256]{2,1,0:T(8,128)(2,1)} %get-tuple-element.7) | data formatting | bytes 2097152
  28.1 0.0 copy-done
  28.1 0.6 %copy.16 = bf16[3,8,256]{2,1,0:T(8,128)(2,1)} copy(bf16[3,8,256]{2,1,0:T(8,128)(2,1)S(1)} %copy-done) | data formatting | bytes 24576
Async XLA Ops:
  23.6 4.5 %copy-start = (bf16[3,8,256]{2,1,0:T(8,128)(2,1)S(1)}, bf16[3,8,256]{2,1,0:T(8,128)(2,1)}, u32[]{:S(2)}) copy-start(bf16[3,8,256]{2,1,0:T(8,128)(2,1)} %get-tuple-element.8) | copy-start | bytes 36868

commit v3 on v2

--- a/solution.py
+++ b/solution.py
@@ -57,7 +57,7 @@
 
 MESH = pl.DeviceIdType.MESH
 STAT_ROWS = 16
-VMEM_BYTES = 64 * 1024 * 1024
+VMEM_BYTES = 32 * 1024 * 1024
 
 
 def new_rows(old, slots, rows_f32, step_rows):
@@ -70,9 +70,9 @@
 
 def fused_kernel(
     n_ctx, n_head, steps, batch, groups, kv_local,
-    fill, owner, q_hbm, k_hbm, v_hbm, nk_hbm, nv_hbm, w_hbm,
+    fill_hbm, owner_hbm, q_hbm, k_hbm, v_hbm, nk_hbm, nv_hbm, w_hbm,
     k_out, v_out, mixed,
-    q_v, nk_v, nv_v, k_v, v_v, w_v, q_rows, part, stat, nk_f, nv_f,
+    fill, owner, q_v, nk_v, nv_v, k_v, v_v, w_v, q_rows, part, stat, nk_f, nv_f,
     send1, recv1, send2, recv2, send3, recv3,
     small_sem, k_sem, v_sem, w_sem, ko_sem, vo_sem,
     ssem1, rsem1, ssem2, rsem2, ssem3, rsem3,
@@ -97,6 +97,8 @@
         pltpu.make_async_copy(q_hbm, q_v, small_sem.at[0]),
         pltpu.make_async_copy(nk_hbm, nk_v, small_sem.at[1]),
         pltpu.make_async_copy(nv_hbm, nv_v, small_sem.at[2]),
+        pltpu.make_async_copy(fill_hbm, fill, small_sem.at[3]),
+        pltpu.make_async_copy(owner_hbm, owner, small_sem.at[4]),
     ]
     k_in = [pltpu.make_async_copy(k_hbm.at[b], k_v.at[b], k_sem.at[b]) for b in range(batch)]
     v_in = [pltpu.make_async_copy(v_hbm.at[b], v_v.at[b], v_sem.at[b]) for b in range(batch)]
@@ -132,6 +134,8 @@
         == lax.broadcasted_iota(jnp.int32, (STAT_ROWS, HD), 1)
     ).astype(jnp.bfloat16)
 
+    smalls[3].wait()
+    smalls[4].wait()
     slots, lengths = [], []
     for b in range(batch):
         seen = fill[b]
@@ -301,6 +305,18 @@
         copy.wait()
 
 
+def write_kernel(k_in, v_in, m_in, k_out, v_out, m_out, sems):
+    batch = k_in.shape[0]
+    copies = [pltpu.make_async_copy(m_in, m_out, sems.at[2 * batch])]
+    for b in range(batch):
+        copies.append(pltpu.make_async_copy(k_in.at[b], k_out.at[b], sems.at[b]))
+        copies.append(pltpu.make_async_copy(v_in.at[b], v_out.at[b], sems.at[batch + b]))
+    for copy in copies:
+        copy.start()
+    for copy in copies:
+        copy.wait()
+
+
 def on_device_fused(
     n_ctx, n_head, queries, k_cache, v_cache, new_keys, new_values, fill, owner, out_weight
 ):
@@ -320,18 +336,20 @@
         fused_kernel, n_ctx, n_head, steps, batch, heads // kv_local, kv_local
     )
     whole = pl.BlockSpec(memory_space=pl.ANY)
-    scalars = pl.BlockSpec(memory_space=pltpu.SMEM)
     dma = pltpu.SemaphoreType.DMA
-    return pl.pallas_call(
+    shapes = (
+        jax.ShapeDtypeStruct(k_cache.shape, k_cache.dtype),
+        jax.ShapeDtypeStruct(v_cache.shape, v_cache.dtype),
+        jax.ShapeDtypeStruct((steps, batch, columns // n_head), jnp.bfloat16),
+    )
+    results = pl.pallas_call(
         kernel,
-        out_shape=(
-            jax.ShapeDtypeStruct(k_cache.shape, k_cache.dtype),
-            jax.ShapeDtypeStruct(v_cache.shape, v_cache.dtype),
-            jax.ShapeDtypeStruct((steps, batch, columns // n_head), jnp.bfloat16),
-        ),
-        in_specs=[scalars, scalars] + [whole] * 6,
+        out_shape=shapes,
+        in_specs=[whole] * 8,
         out_specs=(whole, whole, pl.BlockSpec(memory_space=pltpu.VMEM)),
         scratch_shapes=[
+            pltpu.SMEM((batch,), jnp.int32),
+            pltpu.SMEM((steps, batch), jnp.int32),
             pltpu.VMEM(queries.shape, jnp.bfloat16),
             pltpu.VMEM(new_keys.shape, jnp.bfloat16),
             pltpu.VMEM(new_values.shape, jnp.bfloat16),
@@ -349,7 +367,7 @@
             pltpu.VMEM((n_ctx, block, HD), jnp.bfloat16),
             pltpu.VMEM((n_head, tokens, columns // n_head), jnp.float32),
             pltpu.VMEM((n_head, tokens, columns // n_head), jnp.float32),
-            dma((3,)),
+            dma((5,)),
             dma((batch,)),
             dma((batch,)),
             dma((n_ctx,)),
@@ -370,7 +388,20 @@
             bytes_accessed=2 * (2 * k_cache.size + 2 * v_cache.size + out_weight.size),
             transcendentals=tokens * heads * rows,
         ),
-    )(fill.reshape(batch), owner, queries, k_cache, v_cache, new_keys, new_values, out_weight)
+    )(*[
+        pltpu.with_memory_space_constraint(x, pltpu.HBM)
+        for x in (
+            fill.reshape(batch), owner, queries, k_cache, v_cache, new_keys, new_values, out_weight
+        )
+    ])
+    return pl.pallas_call(
+        write_kernel,
+        out_shape=shapes,
+        in_specs=[whole] * 3,
+        out_specs=(whole,) * 3,
+        scratch_shapes=[dma((2 * batch + 1,))],
+        compiler_params=pltpu.CompilerParams(vmem_limit_bytes=1024 * 1024),
+    )(*[pltpu.with_memory_space_constraint(x, pltpu.VMEM) for x in results])
 
 
 def solution(mesh):

time: 28.9 us -> 23.9 us (0.83)
  local copies, waits for them, and re-layouts: 5.13 us -> 0 us
    unnamed x5 -> x0, local copies, waits for them, and re-layouts: 5.13 us -> none
    pallas_call x1 -> x2, Pallas kernels: 23 us -> 23.1 us  [the longest x1 21.7 us: on_device_fused(): pl.pallas_call(kernel, out_shape=shapes, in_specs=[whole] * 8, out_specs=...]
where the time goes in v3:
time: 23.9 us; the launch traced here: 23.8 us
  Pallas kernels  23.1 us (97%)
  between operations  0.64 us (3%)
    pallas_call x1, Pallas kernels, on_device_fused(): pl.pallas_call(kernel, out_shape=shapes, in_specs=[whole] * 8, out_specs=...  21.7 us
    pallas_call x1, Pallas kernels, on_device_fused(): pl.pallas_call(write_kernel, out_shape=shapes, in_specs=[whole] * 3, out_...  1.45 us

profile of v3, /device:TPU:0, one launch (start us, length us, event | category | flops | bytes accessed | tf_op | source)
XLA Modules:
  0.0 23.8 jit_solution(6518015002626112854)
XLA Ops:
  0.6 21.7 %shard_map.103 = (bf16[8,256,256]{2,1,0:T(8,128)(2,1)S(1)}, bf16[8,256,256]{2,1,0:T(8,128)(2,1)S(1)}, bf16[3,8,256]{2,1,0:T(8,128)(2,1)S(1)}) custom-call(s32[8]{0:T(128)} %bitcast.1, s32[3,8]{1,0:T(4,128)} %owner_hbm.1, bf16[3,8,2048]{2,1,0:T(8,128)(2,1)} %q_hbm.1, bf16[8,256,256]{2,1,0:T(8,128)(2,1)} %k_hbm.1, bf16[8,256,256]{2,1,0:T(8,128)(2,1)} %v_hbm.1, ...), custom_call_target="tpu_custom_call" | custom-call | flops 150994944 | bytes 8388608 | tf_op jit(solution)/shard_map/pallas_call | solution.py:345
  22.3 1.5 %shard_map.104 = (bf16[8,256,256]{2,1,0:T(8,128)(2,1)}, bf16[8,256,256]{2,1,0:T(8,128)(2,1)}, bf16[3,8,256]{2,1,0:T(8,128)(2,1)}) custom-call(bf16[8,256,256]{2,1,0:T(8,128)(2,1)S(1)} %get-tuple-element.6.k_in, bf16[8,256,256]{2,1,0:T(8,128)(2,1)S(1)} %get-tuple-element.7.v_in, bf16[3,8,256]{2,1,0:T(8,128)(2,1)S(1)} %get-tuple-element.8.m_in), custom_call_target="tpu_custom_call" | custom-call | tf_op jit(solution)/shard_map/pallas_call | solution.py:397

commit v4 on v3

--- a/solution.py
+++ b/solution.py
@@ -87,12 +87,6 @@
     depth = per * HD
     width = mixed.shape[2]
 
-    barrier = pltpu.get_barrier_semaphore()
-    for d in range(1, n_ctx):
-        pl.semaphore_signal(barrier, inc=1, device_id={"ctx": lax.rem(me + d, n_ctx)}, device_id_type=MESH)
-    for d in range(1, n_head):
-        pl.semaphore_signal(barrier, inc=1, device_id={"head": lax.rem(hme + d, n_head)}, device_id_type=MESH)
-
     smalls = [
         pltpu.make_async_copy(q_hbm, q_v, small_sem.at[0]),
         pltpu.make_async_copy(nk_hbm, nk_v, small_sem.at[1]),
@@ -106,13 +100,19 @@
         pltpu.make_async_copy(w_hbm.at[pl.ds(c * depth, depth), :], w_v.at[c], w_sem.at[c])
         for c in range(n_ctx)
     ]
-    for copy in smalls:
+    smalls[0].start()
+    for copy in k_in:
         copy.start()
-    for b in range(batch):
-        k_in[b].start()
-        v_in[b].start()
-    for copy in w_in:
+    for copy in smalls[1:]:
         copy.start()
+    for copy in v_in:
+        copy.start()
+
+    barrier = pltpu.get_barrier_semaphore()
+    for d in range(1, n_ctx):
+        pl.semaphore_signal(barrier, inc=1, device_id={"ctx": lax.rem(me + d, n_ctx)}, device_id_type=MESH)
+    for d in range(1, n_head):
+        pl.semaphore_signal(barrier, inc=1, device_id={"head": lax.rem(hme + d, n_head)}, device_id_type=MESH)
 
     smalls[0].wait()
     for s in range(steps):
@@ -121,14 +121,17 @@
             q_rows[h * tokens + s * batch : h * tokens + (s + 1) * batch, :] = q_f[:, h * HD : (h + 1) * HD]
     smalls[1].wait()
     smalls[2].wait()
+    nk_f[...] = jnp.zeros_like(nk_f)
+    nv_f[...] = jnp.zeros_like(nv_f)
     for s in range(steps):
         nk_f[s * batch : (s + 1) * batch, :] = nk_v[s].astype(jnp.float32)
         nv_f[s * batch : (s + 1) * batch, :] = nv_v[s].astype(jnp.float32)
 
     live_rows = groups * steps
-    step_ids = lax.rem(lax.broadcasted_iota(jnp.int32, (live_rows, rows), 0), steps)
     slot_ids = lax.broadcasted_iota(jnp.int32, (live_rows, rows), 1)
     lane = lax.broadcasted_iota(jnp.int32, (live_rows, HD), 1)
+    even = lax.rem(lane, 2) == 0
+    step_ids = lax.rem(lax.broadcasted_iota(jnp.int32, (live_rows, HD), 0), steps)
     pick = (
         lax.broadcasted_iota(jnp.int32, (STAT_ROWS, HD), 0)
         == lax.broadcasted_iota(jnp.int32, (STAT_ROWS, HD), 1)
@@ -136,17 +139,19 @@
 
     smalls[3].wait()
     smalls[4].wait()
-    slots, lengths = [], []
+    slots = []
+    mine_ids = jnp.full((live_rows, HD), steps, jnp.int32)
     for b in range(batch):
         seen = fill[b]
-        slots_b, lengths_b = [], []
+        slots_b = []
         for s in range(steps):
             mine = owner[s, b] == me
             slots_b.append(jnp.where(mine, seen, -1))
             seen = seen + jnp.where(mine, 1, 0)
-            lengths_b.append(seen)
+            mine_ids = jnp.where(lane == s * batch + b, jnp.where(mine, s, steps), mine_ids)
         slots.append(slots_b)
-        lengths.append(lengths_b)
+    visible = mine_ids <= step_ids
+    new_live = [visible & (lax.rem(lane, batch) == b) for b in range(batch)]
 
     def first(c):
         d = lax.rem(c - me + n_ctx, n_ctx)
@@ -155,50 +160,69 @@
             device_id={"ctx": c}, device_id_type=MESH,
         )
 
-    for b in range(batch):
-        k_in[b].wait()
-    for b in range(batch):
-        v_in[b].wait()
     all_b = range(batch)
     sent = 0
     for g in range(kv_local):
         cols = slice(g * HD, (g + 1) * HD)
-        nk_g, nv_g = nk_f[:, cols], nv_f[:, cols]
+        nk_g = nk_f[:, cols].astype(jnp.bfloat16)
+        nv_g = nv_f[:, cols].astype(jnp.bfloat16)
         at = [pl.ds(g * groups * tokens + b, live_rows, stride=batch) for b in all_b]
-        step_rows = [[s * batch + b for s in range(steps)] for b in all_b]
         query = [q_rows[at[b], :].astype(jnp.bfloat16) for b in all_b]
-        keys = [new_rows(k_v[b, :, cols], slots[b], nk_g, step_rows[b]) for b in all_b]
+        if g == 0:
+            for copy in k_in:
+                copy.wait()
         scores = [
             lax.dot_general(
-                query[b], keys[b], (((1,), (1,)), ((), ())), preferred_element_type=jnp.float32
+                query[b], k_v[b, :, cols], (((1,), (1,)), ((), ())),
+                preferred_element_type=jnp.float32,
             )
             for b in all_b
         ]
-        for b in all_b:
-            k_v[b, :, cols] = keys[b]
-        values = [new_rows(v_v[b, :, cols], slots[b], nv_g, step_rows[b]) for b in all_b]
-        for b in all_b:
-            v_v[b, :, cols] = values[b]
-        live = []
-        for b in all_b:
-            length = jnp.full((live_rows, rows), lengths[b][steps - 1], jnp.int32)
-            for s in range(steps - 1):
-                length = jnp.where(step_ids == s, lengths[b][s], length)
-            live.append(slot_ids < length)
-        masked = [jnp.where(live[b], scores[b] * (1.0 / HD**0.5), -1e30) for b in all_b]
-        peak = [jnp.max(masked[b], axis=1, keepdims=True) for b in all_b]
-        weights = [jnp.where(live[b], jnp.exp(masked[b] - peak[b]), 0.0) for b in all_b]
-        total = [jnp.sum(weights[b], axis=1, keepdims=True) for b in all_b]
+        new_scores = [
+            lax.dot_general(
+                query[b], nk_g, (((1,), (1,)), ((), ())), preferred_element_type=jnp.float32
+            )
+            for b in all_b
+        ]
+        masked = [
+            jnp.where(slot_ids < fill[b], scores[b] * (1.0 / HD**0.5), -1e30) for b in all_b
+        ]
+        new_masked = [
+            jnp.where(new_live[b], new_scores[b] * (1.0 / HD**0.5), -1e30) for b in all_b
+        ]
+        peak = [
+            jnp.maximum(
+                jnp.max(masked[b], axis=1, keepdims=True),
+                jnp.max(new_masked[b], axis=1, keepdims=True),
+            )
+            for b in all_b
+        ]
+        weights = [jnp.exp(masked[b] - peak[b]) for b in all_b]
+        new_weights = [jnp.exp(new_masked[b] - peak[b]) for b in all_b]
+        total = [
+            jnp.sum(weights[b], axis=1, keepdims=True)
+            + jnp.sum(new_weights[b], axis=1, keepdims=True)
+            for b in all_b
+        ]
+        if g == 0:
+            for copy in v_in:
+                copy.wait()
+            for copy in w_in:
+                copy.start()
         sums = [
             jnp.dot(
-                weights[b].astype(jnp.bfloat16), values[b], preferred_element_type=jnp.float32
+                weights[b].astype(jnp.bfloat16), v_v[b, :, cols],
+                preferred_element_type=jnp.float32,
+            )
+            + jnp.dot(
+                new_weights[b].astype(jnp.bfloat16), nv_g, preferred_element_type=jnp.float32
             )
             for b in all_b
         ]
         for b in all_b:
             part[at[b], :] = sums[b]
         for b in all_b:
-            both = jnp.where(lax.rem(lane, 2) == 0, peak[b], total[b])
+            both = jnp.where(even, peak[b], total[b])
             high = both.astype(jnp.bfloat16).astype(jnp.float32)
             middle = (both - high).astype(jnp.bfloat16).astype(jnp.float32)
             low = both - high - middle
@@ -224,8 +248,13 @@
 
     outs = [pltpu.make_async_copy(k_v.at[b], k_out.at[b], ko_sem.at[b]) for b in all_b]
     outs += [pltpu.make_async_copy(v_v.at[b], v_out.at[b], vo_sem.at[b]) for b in all_b]
+    for b in all_b:
+        step_rows = [s * batch + b for s in range(steps)]
+        k_v[b] = new_rows(k_v[b], slots[b], nk_f, step_rows)
+        v_v[b] = new_rows(v_v[b], slots[b], nv_f, step_rows)
     for copy in outs:
         copy.start()
+
     recv1[0] = send1[me]
     for d in range(1, n_ctx):
         pltpu.make_async_remote_copy(
@@ -247,41 +276,47 @@
         attention += recv1[d, 0:block, :].astype(jnp.float32) * shares[:, d : d + 1]
     send2[...] = attention.astype(jnp.bfloat16)
 
-    second = []
-    for d in range(1, n_ctx):
-        copy = pltpu.make_async_remote_copy(
+    seconds = {}
+    for d in sorted(range(1, n_ctx), key=lambda d: -min(d, n_ctx - d)):
+        seconds[d] = pltpu.make_async_remote_copy(
             src_ref=send2, dst_ref=recv2.at[d], send_sem=ssem2.at[d], recv_sem=rsem2.at[d],
             device_id={"ctx": lax.rem(me + d, n_ctx)}, device_id_type=MESH,
         )
-        copy.start()
-        second.append(copy)
+        seconds[d].start()
     for copy in w_in:
         copy.wait()
+    order = [0] + sorted(range(1, n_ctx), key=lambda d: min(d, n_ctx - d))
     share = None
-    for d in range(n_ctx):
+    for d in order:
         if d > 0:
-            second[d - 1].wait_recv()
+            seconds[d].wait_recv()
             got = recv2[d].astype(jnp.float32)
         else:
             got = send2[...].astype(jnp.float32)
         features = jnp.concatenate(
             [got[i * tokens : (i + 1) * tokens] for i in range(per)], axis=1
         ).astype(jnp.bfloat16)
-        product = jnp.dot(
-            features, w_v[lax.rem(me - d + n_ctx, n_ctx)], preferred_element_type=jnp.float32
-        )
+        source = lax.rem(me - d + n_ctx, n_ctx)
+        if d == order[-1]:
+            break
+        product = jnp.dot(features, w_v[source], preferred_element_type=jnp.float32)
         share = product if share is None else share + product
     for h in range(n_head):
         send3[h] = share[:, h * width : (h + 1) * width]
     third = []
-    for d in range(1, n_head):
+    for d in sorted(range(n_head), key=lambda d: -min(d, n_head - d)):
         target = lax.rem(hme + d, n_head)
-        copy = pltpu.make_async_remote_copy(
-            src_ref=send3.at[target], dst_ref=recv3.at[d], send_sem=ssem3.at[d], recv_sem=rsem3.at[d],
-            device_id={"head": target}, device_id_type=MESH,
+        columns = pl.ds(pl.multiple_of(target * width, width), width)
+        send3[target] = send3[target] + jnp.dot(
+            features, w_v[source, :, columns], preferred_element_type=jnp.float32
         )
-        copy.start()
-        third.append(copy)
+        if d > 0:
+            copy = pltpu.make_async_remote_copy(
+                src_ref=send3.at[target], dst_ref=recv3.at[d], send_sem=ssem3.at[d], recv_sem=rsem3.at[d],
+                device_id={"head": target}, device_id_type=MESH,
+            )
+            copy.start()
+            third.append(copy)
     result = send3[hme]
     for copy in third:
         copy.wait_recv()
@@ -297,7 +332,7 @@
         def _(c=c):
             first(c).wait_send()
 
-    for copy in second:
+    for copy in seconds.values():
         copy.wait_send()
     for copy in third:
         copy.wait_send()
@@ -328,7 +363,7 @@
     columns = out_weight.shape[1]
     per = heads // n_ctx
     block = per * tokens
-    if heads % n_ctx or block % 16 or block > HD or n_ctx % kv_local or batch != 8 or columns % (n_head * HD):
+    if heads % n_ctx or block % 16 or block > HD or n_ctx % kv_local or batch != 8 or tokens > HD or columns % (n_head * HD):
         return on_device(
             queries, k_cache, v_cache, new_keys, new_values, fill, owner, out_weight
         )
@@ -359,8 +394,8 @@
             pltpu.VMEM((heads * tokens, HD), jnp.float32),
             pltpu.VMEM((heads * tokens, HD), jnp.float32),
             pltpu.VMEM((heads * tokens, HD), jnp.float32),
-            pltpu.VMEM((tokens, kv_width), jnp.float32),
-            pltpu.VMEM((tokens, kv_width), jnp.float32),
+            pltpu.VMEM((HD, kv_width), jnp.float32),
+            pltpu.VMEM((HD, kv_width), jnp.float32),
             pltpu.VMEM((n_ctx, block + STAT_ROWS, HD), jnp.bfloat16),
             pltpu.VMEM((n_ctx, block + STAT_ROWS, HD), jnp.bfloat16),
             pltpu.VMEM((block, HD), jnp.bfloat16),

time: 23.9 us -> 24 us (level)
  no operation moved by 1% of the time
where the time goes in v4:
time: 24 us; the launch traced here: 23.8 us
  Pallas kernels  23.2 us (97%)
  between operations  0.64 us (3%)
    pallas_call x1, Pallas kernels, on_device_fused(): pl.pallas_call(kernel, out_shape=shapes, in_specs=[whole] * 8, out_specs=...  21.7 us
    pallas_call x1, Pallas kernels, on_device_fused(): pl.pallas_call(write_kernel, out_shape=shapes, in_specs=[whole] * 3, out_...  1.45 us

profile of v4, /device:TPU:0, one launch (start us, length us, event | category | flops | bytes accessed | tf_op | source)
XLA Modules:
  0.0 23.8 jit_solution(16011178152077319201)
XLA Ops:
  0.6 21.7 %shard_map.103 = (bf16[8,256,256]{2,1,0:T(8,128)(2,1)S(1)}, bf16[8,256,256]{2,1,0:T(8,128)(2,1)S(1)}, bf16[3,8,256]{2,1,0:T(8,128)(2,1)S(1)}) custom-call(s32[8]{0:T(128)} %bitcast.1, s32[3,8]{1,0:T(4,128)} %owner_hbm.1, bf16[3,8,2048]{2,1,0:T(8,128)(2,1)} %q_hbm.1, bf16[8,256,256]{2,1,0:T(8,128)(2,1)} %k_hbm.1, bf16[8,256,256]{2,1,0:T(8,128)(2,1)} %v_hbm.1, ...), custom_call_target="tpu_custom_call" | custom-call | flops 150994944 | bytes 8388608 | tf_op jit(solution)/shard_map/pallas_call | solution.py:380
  22.4 1.5 %shard_map.104 = (bf16[8,256,256]{2,1,0:T(8,128)(2,1)}, bf16[8,256,256]{2,1,0:T(8,128)(2,1)}, bf16[3,8,256]{2,1,0:T(8,128)(2,1)}) custom-call(bf16[8,256,256]{2,1,0:T(8,128)(2,1)S(1)} %get-tuple-element.6.k_in, bf16[8,256,256]{2,1,0:T(8,128)(2,1)S(1)} %get-tuple-element.7.v_in, bf16[3,8,256]{2,1,0:T(8,128)(2,1)S(1)} %get-tuple-element.8.m_in), custom_call_target="tpu_custom_call" | custom-call | tf_op jit(solution)/shard_map/pallas_call | solution.py:432

commit v5 on v4

--- a/solution.py
+++ b/solution.py
@@ -61,11 +61,12 @@
 
 
 def new_rows(old, slots, rows_f32, step_rows):
-    ids = lax.broadcasted_iota(jnp.int32, old.shape, 0)
-    out = old.astype(jnp.float32)
+    ids = lax.broadcasted_iota(jnp.int32, old.shape, 0).astype(jnp.int16)
     for slot, row in zip(slots, step_rows):
-        out = jnp.where(ids == slot, rows_f32[row : row + 1, :], out)
-    return out.astype(old.dtype)
+        new = jnp.broadcast_to(rows_f32[row : row + 1, :], (16, old.shape[1])).astype(old.dtype)
+        new = jnp.concatenate([new] * (old.shape[0] // 16), axis=0)
+        old = jnp.where(ids == jnp.full(old.shape, slot, jnp.int32).astype(jnp.int16), new, old)
+    return old
 
 
 def fused_kernel(
@@ -74,7 +75,7 @@
     k_out, v_out, mixed,
     fill, owner, q_v, nk_v, nv_v, k_v, v_v, w_v, q_rows, part, stat, nk_f, nv_f,
     send1, recv1, send2, recv2, send3, recv3,
-    small_sem, k_sem, v_sem, w_sem, ko_sem, vo_sem,
+    small_sem, k_sem, v_sem, w_sem,
     ssem1, rsem1, ssem2, rsem2, ssem3, rsem3,
 ):
     me = lax.axis_index("ctx")
@@ -107,6 +108,8 @@
         copy.start()
     for copy in v_in:
         copy.start()
+    for copy in w_in:
+        copy.start()
 
     barrier = pltpu.get_barrier_semaphore()
     for d in range(1, n_ctx):
@@ -207,8 +210,6 @@
         if g == 0:
             for copy in v_in:
                 copy.wait()
-            for copy in w_in:
-                copy.start()
         sums = [
             jnp.dot(
                 weights[b].astype(jnp.bfloat16), v_v[b, :, cols],
@@ -246,14 +247,9 @@
 
         sent = ready
 
-    outs = [pltpu.make_async_copy(k_v.at[b], k_out.at[b], ko_sem.at[b]) for b in all_b]
-    outs += [pltpu.make_async_copy(v_v.at[b], v_out.at[b], vo_sem.at[b]) for b in all_b]
+    own_rows = [[s * batch + b for s in range(steps)] for b in all_b]
     for b in all_b:
-        step_rows = [s * batch + b for s in range(steps)]
-        k_v[b] = new_rows(k_v[b], slots[b], nk_f, step_rows)
-        v_v[b] = new_rows(v_v[b], slots[b], nv_f, step_rows)
-    for copy in outs:
-        copy.start()
+        k_out[b] = new_rows(k_v[b], slots[b], nk_f, own_rows[b])
 
     recv1[0] = send1[me]
     for d in range(1, n_ctx):
@@ -283,6 +279,8 @@
             device_id={"ctx": lax.rem(me + d, n_ctx)}, device_id_type=MESH,
         )
         seconds[d].start()
+    for b in all_b:
+        v_out[b] = new_rows(v_v[b], slots[b], nv_f, own_rows[b])
     for copy in w_in:
         copy.wait()
     order = [0] + sorted(range(1, n_ctx), key=lambda d: min(d, n_ctx - d))
@@ -336,8 +334,6 @@
         copy.wait_send()
     for copy in third:
         copy.wait_send()
-    for copy in outs:
-        copy.wait()
 
 
 def write_kernel(k_in, v_in, m_in, k_out, v_out, m_out, sems):
@@ -381,7 +377,7 @@
         kernel,
         out_shape=shapes,
         in_specs=[whole] * 8,
-        out_specs=(whole, whole, pl.BlockSpec(memory_space=pltpu.VMEM)),
+        out_specs=(pl.BlockSpec(memory_space=pltpu.VMEM),) * 3,
         scratch_shapes=[
             pltpu.SMEM((batch,), jnp.int32),
             pltpu.SMEM((steps, batch), jnp.int32),
@@ -406,8 +402,6 @@
             dma((batch,)),
             dma((batch,)),
             dma((n_ctx,)),
-            dma((batch,)),
-            dma((batch,)),
             dma((n_ctx,)),
             dma((n_ctx,)),
             dma((n_ctx,)),

time: 24 us -> 23.8 us (level)
  no operation moved by 1% of the time
where the time goes in v5:
time: 23.8 us; the launch traced here: 23.7 us
  Pallas kernels  23 us (97%)
  between operations  0.64 us (3%)
    pallas_call x1, Pallas kernels, on_device_fused(): pl.pallas_call(kernel, out_shape=shapes, in_specs=[whole] * 8, out_specs=...  21.6 us
    pallas_call x1, Pallas kernels, on_device_fused(): pl.pallas_call(write_kernel, out_shape=shapes, in_specs=[whole] * 3, out_...  1.45 us

profile of v5, /device:TPU:0, one launch (start us, length us, event | category | flops | bytes accessed | tf_op | source)
XLA Modules:
  0.0 23.7 jit_solution(10956121375664032887)
XLA Ops:
  0.6 21.6 %shard_map.103 = (bf16[8,256,256]{2,1,0:T(8,128)(2,1)S(1)}, bf16[8,256,256]{2,1,0:T(8,128)(2,1)S(1)}, bf16[3,8,256]{2,1,0:T(8,128)(2,1)S(1)}) custom-call(s32[8]{0:T(128)} %bitcast.1, s32[3,8]{1,0:T(4,128)} %owner_hbm.1, bf16[3,8,2048]{2,1,0:T(8,128)(2,1)} %q_hbm.1, bf16[8,256,256]{2,1,0:T(8,128)(2,1)} %k_hbm.1, bf16[8,256,256]{2,1,0:T(8,128)(2,1)} %v_hbm.1, ...), custom_call_target="tpu_custom_call" | custom-call | flops 150994944 | bytes 8388608 | tf_op jit(solution)/shard_map/pallas_call | solution.py:376
  22.2 1.5 %shard_map.104 = (bf16[8,256,256]{2,1,0:T(8,128)(2,1)}, bf16[8,256,256]{2,1,0:T(8,128)(2,1)}, bf16[3,8,256]{2,1,0:T(8,128)(2,1)}) custom-call(bf16[8,256,256]{2,1,0:T(8,128)(2,1)S(1)} %get-tuple-element.6.k_in, bf16[8,256,256]{2,1,0:T(8,128)(2,1)S(1)} %get-tuple-element.7.v_in, bf16[3,8,256]{2,1,0:T(8,128)(2,1)S(1)} %get-tuple-element.8.m_in), custom_call_target="tpu_custom_call" | custom-call | tf_op jit(solution)/shard_map/pallas_call | solution.py:426

commit v6 on v5

--- a/solution.py
+++ b/solution.py
@@ -69,6 +69,15 @@
     return old
 
 
+def partner(index, e, size):
+    total, bit = 0, 1
+    while bit < size:
+        here = lax.rem(lax.div(index, bit), 2)
+        total = total + bit * (1 - here if e // bit % 2 else here)
+        bit *= 2
+    return total
+
+
 def fused_kernel(
     n_ctx, n_head, steps, batch, groups, kv_local,
     fill_hbm, owner_hbm, q_hbm, k_hbm, v_hbm, nk_hbm, nv_hbm, w_hbm,
@@ -156,22 +165,25 @@
     visible = mine_ids <= step_ids
     new_live = [visible & (lax.rem(lane, batch) == b) for b in range(batch)]
 
-    def first(c):
-        d = lax.rem(c - me + n_ctx, n_ctx)
-        return pltpu.make_async_remote_copy(
-            src_ref=send1.at[c], dst_ref=recv1.at[d], send_sem=ssem1.at[c], recv_sem=rsem1.at[d],
-            device_id={"ctx": c}, device_id_type=MESH,
+    peers = [partner(me, e, n_ctx) for e in range(n_ctx)]
+    firsts = [None] + [
+        pltpu.make_async_remote_copy(
+            src_ref=send1.at[e], dst_ref=recv1.at[e], send_sem=ssem1.at[e], recv_sem=rsem1.at[e],
+            device_id={"ctx": peers[e]}, device_id_type=MESH,
         )
-
+        for e in range(1, n_ctx)
+    ]
     all_b = range(batch)
-    sent = 0
-    for g in range(kv_local):
-        cols = slice(g * HD, (g + 1) * HD)
+    far_first = list(range(kv_local))[::-1]
+    per_group = n_ctx // kv_local
+    for turn in far_first:
+        g = partner(lax.div(me, per_group), turn, kv_local)
+        cols = pl.ds(pl.multiple_of(g * HD, HD), HD)
         nk_g = nk_f[:, cols].astype(jnp.bfloat16)
         nv_g = nv_f[:, cols].astype(jnp.bfloat16)
         at = [pl.ds(g * groups * tokens + b, live_rows, stride=batch) for b in all_b]
         query = [q_rows[at[b], :].astype(jnp.bfloat16) for b in all_b]
-        if g == 0:
+        if turn == far_first[0]:
             for copy in k_in:
                 copy.wait()
         scores = [
@@ -207,7 +219,7 @@
             + jnp.sum(new_weights[b], axis=1, keepdims=True)
             for b in all_b
         ]
-        if g == 0:
+        if turn == far_first[0]:
             for copy in v_in:
                 copy.wait()
         sums = [
@@ -228,35 +240,28 @@
             middle = (both - high).astype(jnp.bfloat16).astype(jnp.float32)
             low = both - high - middle
             stat[at[b], :] = jnp.where(lane < 2, high, jnp.where(lane < 4, middle, low))
-        ready = n_ctx * (g + 1) // kv_local
-        for c in range(sent, ready):
-            here = slice(c * block, (c + 1) * block)
-            send1[c, 0:block, :] = part[here, :].astype(jnp.bfloat16)
+        group = range((turn + 1) * per_group - 1, turn * per_group - 1, -1)
+        for e in group:
+            here = pl.ds(pl.multiple_of(peers[e] * block, 8), block)
+            to = send1 if e else recv1
+            to[e, 0:block, :] = part[here, :].astype(jnp.bfloat16)
             turned = lax.dot_general(
                 pick, stat[here, :].astype(jnp.bfloat16), (((1,), (1,)), ((), ())),
                 preferred_element_type=jnp.float32,
             )
-            send1[c, block : block + STAT_ROWS, 0:block] = turned.astype(jnp.bfloat16)
-        if g == 0:
+            to[e, block : block + STAT_ROWS, 0:block] = turned.astype(jnp.bfloat16)
+        if turn == far_first[0]:
             pl.semaphore_wait(barrier, n_ctx + n_head - 2)
-        for c in range(sent, ready):
-
-            @pl.when(me != c)
-            def _(c=c):
-                first(c).start()
-
-        sent = ready
+        for e in group:
+            if e:
+                firsts[e].start()
 
     own_rows = [[s * batch + b for s in range(steps)] for b in all_b]
     for b in all_b:
         k_out[b] = new_rows(k_v[b], slots[b], nk_f, own_rows[b])
 
-    recv1[0] = send1[me]
-    for d in range(1, n_ctx):
-        pltpu.make_async_remote_copy(
-            src_ref=send1.at[0], dst_ref=recv1.at[d], send_sem=ssem1.at[0], recv_sem=rsem1.at[d],
-            device_id={"ctx": lax.rem(me + d, n_ctx)}, device_id_type=MESH,
-        ).wait_recv()
+    for e in range(1, n_ctx):
+        firsts[e].wait_recv()
     peaks, totals = [], []
     for d in range(n_ctx):
         got = recv1[d, block : block + STAT_ROWS, 0:block].astype(jnp.float32)
@@ -273,17 +278,17 @@
     send2[...] = attention.astype(jnp.bfloat16)
 
     seconds = {}
-    for d in sorted(range(1, n_ctx), key=lambda d: -min(d, n_ctx - d)):
+    for d in range(n_ctx - 1, 0, -1):
         seconds[d] = pltpu.make_async_remote_copy(
             src_ref=send2, dst_ref=recv2.at[d], send_sem=ssem2.at[d], recv_sem=rsem2.at[d],
-            device_id={"ctx": lax.rem(me + d, n_ctx)}, device_id_type=MESH,
+            device_id={"ctx": peers[d]}, device_id_type=MESH,
         )
         seconds[d].start()
     for b in all_b:
         v_out[b] = new_rows(v_v[b], slots[b], nv_f, own_rows[b])
     for copy in w_in:
         copy.wait()
-    order = [0] + sorted(range(1, n_ctx), key=lambda d: min(d, n_ctx - d))
+    order = list(range(n_ctx))
     share = None
     for d in order:
         if d > 0:
@@ -294,7 +299,7 @@
         features = jnp.concatenate(
             [got[i * tokens : (i + 1) * tokens] for i in range(per)], axis=1
         ).astype(jnp.bfloat16)
-        source = lax.rem(me - d + n_ctx, n_ctx)
+        source = peers[d]
         if d == order[-1]:
             break
         product = jnp.dot(features, w_v[source], preferred_element_type=jnp.float32)
@@ -324,12 +329,8 @@
     for s in range(steps):
         mixed[s] = result[s * batch : (s + 1) * batch]
 
-    for c in range(n_ctx):
-
-        @pl.when(me != c)
-        def _(c=c):
-            first(c).wait_send()
-
+    for copy in firsts[1:]:
+        copy.wait_send()
     for copy in seconds.values():
         copy.wait_send()
     for copy in third:
@@ -359,7 +360,7 @@
     columns = out_weight.shape[1]
     per = heads // n_ctx
     block = per * tokens
-    if heads % n_ctx or block % 16 or block > HD or n_ctx % kv_local or batch != 8 or tokens > HD or columns % (n_head * HD):
+    if heads % n_ctx or block % 16 or block > HD or n_ctx % kv_local or batch != 8 or n_ctx & (n_ctx - 1) or kv_local & (kv_local - 1) or tokens > HD or columns % (n_head * HD):
         return on_device(
             queries, k_cache, v_cache, new_keys, new_values, fill, owner, out_weight
         )

time: 23.8 us -> 22.4 us (0.941)
  Pallas kernels: 23 us -> 21.6 us
    pallas_call x1, Pallas kernels: 21.6 us -> 20.2 us  [on_device_fused(): pl.pallas_call(kernel, out_shape=shapes, in_specs=[whole] * 8, out_specs=...]
where the time goes in v6:
time: 22.4 us; the launch traced here: 22.3 us
  Pallas kernels  21.6 us (96%)
  between operations  0.64 us (3%)
    pallas_call x1, Pallas kernels, on_device_fused(): pl.pallas_call(kernel, out_shape=shapes, in_specs=[whole] * 8, out_specs=...  20.2 us
    pallas_call x1, Pallas kernels, on_device_fused(): pl.pallas_call(write_kernel, out_shape=shapes, in_specs=[whole] * 3, out_...  1.45 us

profile of v6, /device:TPU:0, one launch (start us, length us, event | category | flops | bytes accessed | tf_op | source)
XLA Modules:
  0.0 22.3 jit_solution(17960922712732362687)
XLA Ops:
  0.6 20.2 %shard_map.103 = (bf16[8,256,256]{2,1,0:T(8,128)(2,1)S(1)}, bf16[8,256,256]{2,1,0:T(8,128)(2,1)S(1)}, bf16[3,8,256]{2,1,0:T(8,128)(2,1)S(1)}) custom-call(s32[8]{0:T(128)} %bitcast.1, s32[3,8]{1,0:T(4,128)} %owner_hbm.1, bf16[3,8,2048]{2,1,0:T(8,128)(2,1)} %q_hbm.1, bf16[8,256,256]{2,1,0:T(8,128)(2,1)} %k_hbm.1, bf16[8,256,256]{2,1,0:T(8,128)(2,1)} %v_hbm.1, ...), custom_call_target="tpu_custom_call" | custom-call | flops 150994944 | bytes 8388608 | tf_op jit(solution)/shard_map/pallas_call | solution.py:377
  20.8 1.5 %shard_map.104 = (bf16[8,256,256]{2,1,0:T(8,128)(2,1)}, bf16[8,256,256]{2,1,0:T(8,128)(2,1)}, bf16[3,8,256]{2,1,0:T(8,128)(2,1)}) custom-call(bf16[8,256,256]{2,1,0:T(8,128)(2,1)S(1)} %get-tuple-element.6.k_in, bf16[8,256,256]{2,1,0:T(8,128)(2,1)S(1)} %get-tuple-element.7.v_in, bf16[3,8,256]{2,1,0:T(8,128)(2,1)S(1)} %get-tuple-element.8.m_in), custom_call_target="tpu_custom_call" | custom-call | tf_op jit(solution)/shard_map/pallas_call | solution.py:427

commit v7 on v6

--- a/solution.py
+++ b/solution.py
@@ -83,7 +83,7 @@
     fill_hbm, owner_hbm, q_hbm, k_hbm, v_hbm, nk_hbm, nv_hbm, w_hbm,
     k_out, v_out, mixed,
     fill, owner, q_v, nk_v, nv_v, k_v, v_v, w_v, q_rows, part, stat, nk_f, nv_f,
-    send1, recv1, send2, recv2, send3, recv3,
+    send1, recv1, send2, recv2, send3, recv3, send4, recv4,
     small_sem, k_sem, v_sem, w_sem,
     ssem1, rsem1, ssem2, rsem2, ssem3, rsem3,
 ):
@@ -307,24 +307,36 @@
     for h in range(n_head):
         send3[h] = share[:, h * width : (h + 1) * width]
     third = []
-    for d in sorted(range(n_head), key=lambda d: -min(d, n_head - d)):
-        target = lax.rem(hme + d, n_head)
+    for e in range(n_head - 1, -1, -1):
+        target = partner(hme, e, n_head)
         columns = pl.ds(pl.multiple_of(target * width, width), width)
-        send3[target] = send3[target] + jnp.dot(
+        value = send3[target] + jnp.dot(
             features, w_v[source, :, columns], preferred_element_type=jnp.float32
         )
-        if d > 0:
-            copy = pltpu.make_async_remote_copy(
-                src_ref=send3.at[target], dst_ref=recv3.at[d], send_sem=ssem3.at[d], recv_sem=rsem3.at[d],
-                device_id={"head": target}, device_id_type=MESH,
-            )
-            copy.start()
-            third.append(copy)
-    result = send3[hme]
+        if e == 0:
+            result = value
+            continue
+        if e == 1:
+            send3[target] = value
+            origin, landing = send3.at[target], recv3
+        else:
+            stacked = [value[:, i * HD : (i + 1) * HD] for i in range(width // HD)]
+            send4[e] = jnp.concatenate(stacked, axis=0).astype(jnp.bfloat16)
+            origin, landing = send4.at[e], recv4.at[e]
+        copy = pltpu.make_async_remote_copy(
+            src_ref=origin, dst_ref=landing, send_sem=ssem3.at[e], recv_sem=rsem3.at[e],
+            device_id={"head": target}, device_id_type=MESH,
+        )
+        copy.start()
+        third.append(copy)
     for copy in third:
         copy.wait_recv()
-    for d in range(1, n_head):
-        result += recv3[d]
+    result += recv3[...]
+    for e in range(2, n_head):
+        got = recv4[e].astype(jnp.float32)
+        result += jnp.concatenate(
+            [got[i * tokens : (i + 1) * tokens] for i in range(width // HD)], axis=1
+        )
     result = result.astype(mixed.dtype)
     for s in range(steps):
         mixed[s] = result[s * batch : (s + 1) * batch]
@@ -360,7 +372,7 @@
     columns = out_weight.shape[1]
     per = heads // n_ctx
     block = per * tokens
-    if heads % n_ctx or block % 16 or block > HD or n_ctx % kv_local or batch != 8 or n_ctx & (n_ctx - 1) or kv_local & (kv_local - 1) or tokens > HD or columns % (n_head * HD):
+    if heads % n_ctx or block % 16 or block > HD or n_ctx % kv_local or batch != 8 or n_ctx & (n_ctx - 1) or n_head & (n_head - 1) or n_head < 2 or kv_local & (kv_local - 1) or tokens > HD or columns % (n_head * HD):
         return on_device(
             queries, k_cache, v_cache, new_keys, new_values, fill, owner, out_weight
         )
@@ -398,7 +410,9 @@
             pltpu.VMEM((block, HD), jnp.bfloat16),
             pltpu.VMEM((n_ctx, block, HD), jnp.bfloat16),
             pltpu.VMEM((n_head, tokens, columns // n_head), jnp.float32),
-            pltpu.VMEM((n_head, tokens, columns // n_head), jnp.float32),
+            pltpu.VMEM((tokens, columns // n_head), jnp.float32),
+            pltpu.VMEM((n_head, tokens * columns // n_head // HD, HD), jnp.bfloat16),
+            pltpu.VMEM((n_head, tokens * columns // n_head // HD, HD), jnp.bfloat16),
             dma((5,)),
             dma((batch,)),
             dma((batch,)),

time: 22.4 us -> 22.4 us (level)
  no operation moved by 1% of the time
where the time goes in v7:
time: 22.4 us; the launch traced here: 22.3 us
  Pallas kernels  21.6 us (96%)
  between operations  0.64 us (3%)
    pallas_call x1, Pallas kernels, on_device_fused(): pl.pallas_call(kernel, out_shape=shapes, in_specs=[whole] * 8, out_specs=...  20.2 us
    pallas_call x1, Pallas kernels, on_device_fused(): pl.pallas_call(write_kernel, out_shape=shapes, in_specs=[whole] * 3, out_...  1.45 us

profile of v7, /device:TPU:0, one launch (start us, length us, event | category | flops | bytes accessed | tf_op | source)
XLA Modules:
  0.0 22.3 jit_solution(17135993494614114361)
XLA Ops:
  0.6 20.2 %shard_map.103 = (bf16[8,256,256]{2,1,0:T(8,128)(2,1)S(1)}, bf16[8,256,256]{2,1,0:T(8,128)(2,1)S(1)}, bf16[3,8,256]{2,1,0:T(8,128)(2,1)S(1)}) custom-call(s32[8]{0:T(128)} %bitcast.1, s32[3,8]{1,0:T(4,128)} %owner_hbm.1, bf16[3,8,2048]{2,1,0:T(8,128)(2,1)} %q_hbm.1, bf16[8,256,256]{2,1,0:T(8,128)(2,1)} %k_hbm.1, bf16[8,256,256]{2,1,0:T(8,128)(2,1)} %v_hbm.1, ...), custom_call_target="tpu_custom_call" | custom-call | flops 150994944 | bytes 8388608 | tf_op jit(solution)/shard_map/pallas_call | solution.py:389
  20.8 1.5 %shard_map.104 = (bf16[8,256,256]{2,1,0:T(8,128)(2,1)}, bf16[8,256,256]{2,1,0:T(8,128)(2,1)}, bf16[3,8,256]{2,1,0:T(8,128)(2,1)}) custom-call(bf16[8,256,256]{2,1,0:T(8,128)(2,1)S(1)} %get-tuple-element.6.k_in, bf16[8,256,256]{2,1,0:T(8,128)(2,1)S(1)} %get-tuple-element.7.v_in, bf16[3,8,256]{2,1,0:T(8,128)(2,1)S(1)} %get-tuple-element.8.m_in), custom_call_target="tpu_custom_call" | custom-call | tf_op jit(solution)/shard_map/pallas_call | solution.py:441
